TPU v7x, 32 devices: a whole 2x2x4 slice. The times are simulated.
32 devices in a mesh: dp: 4 (over x, core), ctx: 8 (over z, y).
Axes of the slice: x: 2, y: 2, z: 4, core: 2. Of those that a mesh axis runs over, the one named last changes fastest.
Arguments:
- gate_input: bfloat16 [4, 1024, 4096], P('dp', 'ctx'), may hold values from -6 to 6
- values: bfloat16 [4, 1024, 4096], P('dp', 'ctx'), may hold values from -6 to 6
- cotangent: bfloat16 [4, 1024, 4096], P('dp', 'ctx'), may hold values from -6 to 6
- filter_taps: float32 [1024, 4096], P(('dp', 'ctx')), may hold values from -4 to 4
Outputs:
- output: bfloat16 [4, 1024, 4096], P('dp', 'ctx')
- gate_grad: bfloat16 [4, 1024, 4096], P('dp', 'ctx')
- values_grad: bfloat16 [4, 1024, 4096], P('dp', 'ctx')
- filter_grad: float32 [1024, 4096], P(('dp', 'ctx'))
All inputs are finite; a program needn't handle non-finite values.
Results may differ from a plain program's by a relative error of at most 0.013.
Values may be sent and summed in bfloat16 or wider, within the bound.
A program may use at most 128 MiB of HBM per device.

v0:
```python
import functools
import math

import jax
import jax.numpy as jnp
import numpy as np
from jax import lax
from jax.experimental import pallas as pl
from jax.experimental.pallas import tpu as pltpu
from jax.sharding import PartitionSpec as P

MESH = pl.DeviceIdType.MESH
WIDTH = 256
TABLE_LIMIT = 8 * 2**20
TILE = 256
OUTER_EIGHTHS = 2


def odd_tables(seq_len):
    turns = np.outer(2 * np.arange(seq_len) + 1, np.arange(seq_len)) % (4 * seq_len)
    angles = turns * (2.0 * math.pi / (4 * seq_len))
    forward = np.concatenate([np.cos(angles), -np.sin(angles)], axis=0)
    inverse = forward.T / seq_len
    forward = np.stack([forward[:, : seq_len // 2], forward[:, seq_len // 2 :]])
    return jnp.asarray(forward, jnp.bfloat16), jnp.asarray(inverse, jnp.bfloat16)


def dot(left, right):
    return jnp.dot(left, right, preferred_element_type=jnp.float32)


def loop(first, last, body):
    def step(index, carry):
        body(index)
        return carry

    lax.fori_loop(first, last, step, 0)


def kernel(
    dims,
    gate_hbm, values_hbm, cot_hbm, taps_hbm, forward_hbm, inverse_hbm,
    out_ref, gate_grad_ref, values_grad_ref, filter_grad_ref,
    gate, cot, taps, forward, inverse, taps_half, signal_rows,
    near, whole, taps_cols, mixed_near, mixed_far, mixed_taps,
    near_cols, far_cols, partial, partial_in, summed, result_rows, summed_rows,
    load_sem, gather_sem, reduce_sem,
    near_sem, cross_sem, far_sem, taps_sem, taps_cross_sem, back_near_sem, back_far_sem,
    summed_sem, summed_cross_sem,
):
    ctx, dp, rows, seq_len, outer, inner = dims
    side = ctx // 2
    most = max(outer, inner)
    part = seq_len // dp
    own_rows = part // ctx
    half_len = seq_len // 2
    me = lax.axis_index("ctx")
    group = lax.axis_index("dp")
    half = me // side
    place = lax.rem(me, side)
    low = half == 0
    early = group * part < half_len

    def counts(owner):
        first = outer + (owner // side) * (inner - outer)
        second = outer + inner - first
        return first, second, lax.rem(owner, side) // (side // 2)

    def count(owner):
        first, second, late = counts(owner)
        return first + late * (second - first)

    def columns(owner, chunk):
        first, second, late = counts(owner)
        at = lax.rem(owner, side)
        early_at = at - late * (at - side // 2)
        base = early_at * first + (at - early_at) * second
        return pl.ds(pl.multiple_of((base + chunk) * WIDTH, WIDTH), WIDTH)

    def block(index, size):
        return pl.ds(pl.multiple_of(index * size, size), size)

    def remote(src, dst, send_sem, recv_sem, device):
        return pltpu.make_async_remote_copy(
            src_ref=src, dst_ref=dst, send_sem=send_sem, recv_sem=recv_sem,
            device_id=device, device_id_type=MESH,
        )

    def peer_at(offset, crossing):
        where = lax.rem(place + offset + side, side)
        return (1 - half if crossing else half) * side + where

    class Exchange:
        def __init__(self, refs, sems, crossing, inbound):
            self.refs, self.sems, self.crossing, self.inbound = refs, sems, crossing, inbound

        def own(self, chunk):
            source, target = self.refs(chunk, me, me)
            return pltpu.make_async_copy(source, target, self.sems.at[1, chunk, 0])

        def to(self, chunk, offset):
            peer = peer_at(offset, self.crossing)
            source, target = self.refs(chunk, me, peer)
            return remote(source, target, self.sems.at[0, chunk, offset],
                          self.sems.at[1, chunk, offset], {"ctx": peer})

        def back(self, chunk, offset):
            peer = peer_at(-offset, self.crossing)
            source, target = self.refs(chunk, peer, me)
            return remote(source, target, self.sems.at[0, chunk, offset],
                          self.sems.at[1, chunk, offset], {"ctx": peer})

        def each(self, chunk, sending, act):
            def one(offset):
                peer = peer_at(offset if sending else -offset, self.crossing)
                counted = peer if sending == self.inbound else me

                @pl.when(chunk < count(counted))
                def _():
                    act(offset)

            loop(0 if self.crossing else 1, side, one)

        def start(self, chunk):
            self.each(chunk, True, lambda offset: self.to(chunk, offset).start())
            if not self.crossing:
                @pl.when(chunk < count(me))
                def _():
                    self.own(chunk).start()

        def arrive(self, chunk):
            self.each(chunk, False, lambda offset: self.back(chunk, offset).wait_recv())
            if not self.crossing:
                @pl.when(chunk < count(me))
                def _():
                    self.own(chunk).wait()

        def leave(self, chunk):
            self.each(chunk, True, lambda offset: self.to(chunk, offset).wait_send())

    def near_refs(chunk, sender, receiver):
        return (signal_rows.at[0, :, columns(receiver, chunk)],
                near.at[chunk, block(lax.rem(sender, side), rows), :])

    def cross_refs(chunk, sender, receiver):
        return (signal_rows.at[0, :, columns(receiver, chunk)],
                whole.at[chunk, block(sender, rows), :])

    def far_refs(chunk, sender, receiver):
        return (signal_rows.at[1, :, columns(receiver, chunk)],
                whole.at[chunk, block(sender, rows), :])

    def taps_refs(chunk, sender, receiver):
        return (taps_half.at[:, columns(receiver, chunk)],
                taps_cols.at[chunk, block(group * ctx + sender, own_rows), :])

    def back_near_refs(chunk, sender, receiver):
        return (near_cols.at[chunk, block(lax.rem(receiver, side), rows), :],
                result_rows.at[half, :, columns(sender, chunk)])

    def back_far_refs(chunk, sender, receiver):
        return (far_cols.at[chunk, block(lax.rem(receiver, side), rows), :],
                result_rows.at[1 - half, :, columns(sender, chunk)])

    def summed_refs(chunk, sender, receiver):
        return (summed.at[chunk, block(receiver, own_rows), :],
                summed_rows.at[sender // side, :, columns(sender, chunk)])

    near_way = Exchange(near_refs, near_sem, False, True)
    cross_way = Exchange(cross_refs, cross_sem, True, True)
    far_way = Exchange(far_refs, far_sem, False, True)
    taps_way = Exchange(taps_refs, taps_sem, False, True)
    taps_cross_way = Exchange(taps_refs, taps_cross_sem, True, True)
    back_near_way = Exchange(back_near_refs, back_near_sem, False, False)
    back_far_way = Exchange(back_far_refs, back_far_sem, False, False)
    summed_way = Exchange(summed_refs, summed_sem, False, False)
    summed_cross_way = Exchange(summed_refs, summed_cross_sem, True, False)

    loads = [
        pltpu.make_async_copy(src, dst, load_sem.at[at])
        for at, (src, dst) in enumerate(
            [(taps_hbm, taps), (values_hbm, signal_rows.at[half]), (gate_hbm, gate),
             (cot_hbm, cot), (forward_hbm, forward), (inverse_hbm, inverse)]
        )
    ]
    for load in loads:
        load.start()

    barrier = pltpu.get_barrier_semaphore()
    loop(1, ctx, lambda offset: pl.semaphore_signal(
        barrier, inc=1, device_id={"ctx": lax.rem(me + offset, ctx)}, device_id_type=MESH))
    loop(1, dp, lambda offset: pl.semaphore_signal(
        barrier, inc=1, device_id={"dp": lax.rem(group + offset, dp)}, device_id_type=MESH))
    loads[0].wait()
    taps_half[...] = taps[...].astype(jnp.bfloat16)
    loads[2].wait()
    loads[3].wait()

    def grad_band(index):
        band = block(index, 16)
        product = gate[band, :].astype(jnp.float32) * cot[band, :].astype(jnp.float32)
        signal_rows[1 - half, band, :] = product.astype(jnp.bfloat16)

    loop(0, rows // 16, grad_band)
    loads[1].wait()
    pl.semaphore_wait(barrier, ctx + dp - 2)

    def send_in(chunk):
        taps_cross_way.start(chunk)
        taps_way.start(chunk)
        cross_way.start(chunk)
        near_way.start(chunk)
        far_way.start(chunk)

    loop(0, most, send_in)
    mine = count(me)

    def gathered(chunk, offset, owner):
        peer = lax.rem(group + offset, dp)
        held = taps_cols.at[chunk, block(owner, part), :]
        return remote(held, held, gather_sem.at[0, chunk, offset], gather_sem.at[1, chunk, offset],
                      {"dp": peer})

    def gather(chunk):
        taps_cross_way.arrive(chunk)
        taps_way.arrive(chunk)
        loop(1, dp, lambda offset: gathered(chunk, offset, group).start())

    loop(0, mine, gather)
    loads[4].wait()
    loads[5].wait()
    sign = jnp.where(low, 1.0, -1.0).astype(jnp.float32)
    keep = jnp.where(low, 1.0, 0.0).astype(jnp.float32)

    def reduces(owner):
        return jnp.logical_or(low, owner * part < half_len)

    def reduced(chunk, offset, owner):
        return remote(
            partial.at[chunk, block(owner, part), :], partial_in.at[chunk, offset],
            reduce_sem.at[0, chunk, offset], reduce_sem.at[1, chunk, offset],
            {"dp": lax.rem(group + offset, dp)})

    def reduce_each(chunk, act):
        def one(offset):
            owner = lax.rem(group + offset, dp)

            @pl.when(reduces(owner))
            def _():
                act(reduced(chunk, offset, owner))

        loop(1, dp, one)

    def finish(chunk):
        @pl.when(reduces(group))
        def _():
            loop(1, dp, lambda offset: reduced(chunk, offset, group).wait_recv())
            total = partial[chunk, block(group, part), :].astype(jnp.float32)
            for offset in range(1, dp):
                total = total + partial_in[chunk, offset].astype(jnp.float32)
            summed[chunk] = total.astype(jnp.bfloat16)
            summed_cross_way.start(chunk)
            summed_way.start(chunk)

    def work(chunk):
        cross_way.arrive(chunk)
        near_way.arrive(chunk)
        far_way.arrive(chunk)
        loop(1, dp, lambda offset: gathered(
            chunk, offset, lax.rem(group + dp - offset, dp)).wait_recv())
        first, second = pl.ds(0, half_len), pl.ds(half_len, half_len)

        def frequencies(index):
            upper = block(index, TILE)
            lower = pl.ds(pl.multiple_of(seq_len + index * TILE, TILE), TILE)

            def split(band):
                taps_part = dot(forward[0, band, :], taps_cols[chunk, first, :]) + dot(
                    forward[1, band, :], taps_cols[chunk, second, :])
                near_part = dot(forward[half, band, :], near[chunk])
                return (taps_part, near_part, dot(forward[0, band, :], whole[chunk, first, :]),
                        dot(forward[1, band, :], whole[chunk, second, :]))

            taps_real, near_real, early_real, late_real = split(upper)
            taps_imag, near_imag, early_imag, late_imag = split(lower)
            taps_imag = taps_imag * sign
            far_real, far_imag = early_real + late_real, early_imag + late_imag
            half_type = jnp.bfloat16
            mixed_near[upper, :] = (near_real * taps_real - near_imag * taps_imag).astype(half_type)
            mixed_near[lower, :] = (near_real * taps_imag + near_imag * taps_real).astype(half_type)
            mixed_far[upper, :] = (far_real * taps_real + far_imag * taps_imag).astype(half_type)
            mixed_far[lower, :] = (far_imag * taps_real - far_real * taps_imag).astype(half_type)
            part_real, part_imag = early_real * keep + late_real, early_imag * keep + late_imag
            mixed_taps[upper, :] = (part_real * near_real + part_imag * near_imag).astype(half_type)
            mixed_taps[lower, :] = (
                (part_imag * near_real - part_real * near_imag) * sign).astype(half_type)

        loop(0, seq_len // TILE, frequencies)

        def inverse_rows(index):
            return inverse[pl.ds(pl.multiple_of(half * half_len + index * TILE, TILE), TILE), :]

        def near_tile(index):
            near_cols[chunk, block(index, TILE), :] = dot(
                inverse_rows(index), mixed_near[...]).astype(jnp.bfloat16)

        def far_tile(index):
            far_cols[chunk, block(index, TILE), :] = dot(
                inverse_rows(index), mixed_far[...]).astype(jnp.bfloat16)

        def taps_tile(index):
            band = block(index, TILE)
            partial[chunk, band, :] = dot(inverse[band, :], mixed_taps[...]).astype(jnp.bfloat16)

        loop(0, half_len // TILE, near_tile)
        back_near_way.start(chunk)
        loop(0, (2 - half) * (half_len // TILE), taps_tile)
        reduce_each(chunk, lambda copy: copy.start())
        loop(0, half_len // TILE, far_tile)
        back_far_way.start(chunk)

        @pl.when(chunk > 0)
        def _():
            finish(chunk - 1)

    loop(0, mine, work)
    finish(mine - 1)

    def results(chunk):
        back_near_way.arrive(chunk)
        back_far_way.arrive(chunk)

    loop(0, most, results)

    def gate_band(index):
        band = block(index, 16)
        conv = result_rows[0, band, :].astype(jnp.float32)
        out_ref[band, :] = (gate[band, :].astype(jnp.float32) * conv).astype(jnp.bfloat16)
        gate_grad_ref[band, :] = (cot[band, :].astype(jnp.float32) * conv).astype(jnp.bfloat16)

    loop(0, rows // 16, gate_band)
    values_grad_ref[...] = result_rows[1]

    @pl.when(low)
    def _():
        loop(0, most, summed_way.arrive)

    @pl.when(jnp.logical_not(low))
    def _():
        loop(0, most, summed_cross_way.arrive)

    filter_grad_ref[...] = summed_rows[0].astype(jnp.float32)

    @pl.when(early)
    def _():
        @pl.when(low)
        def _():
            loop(0, most, summed_cross_way.arrive)

        @pl.when(jnp.logical_not(low))
        def _():
            loop(0, most, summed_way.arrive)

        filter_grad_ref[...] += summed_rows[1].astype(jnp.float32)

    def sent(chunk):
        for way in (taps_cross_way, taps_way, cross_way, near_way, far_way,
                    back_near_way, back_far_way):
            way.leave(chunk)

    loop(0, most, sent)

    def sent_sums(chunk):
        loop(1, dp, lambda offset: gathered(chunk, offset, group).wait_send())
        reduce_each(chunk, lambda copy: copy.wait_send())

        @pl.when(reduces(group))
        def _():
            summed_cross_way.leave(chunk)
            summed_way.leave(chunk)

    loop(0, mine, sent_sums)


def in_one_kernel(gate_input, values, cotangent, filter_taps):
    ctx = lax.axis_size("ctx")
    dp = lax.axis_size("dp")
    rows, channels = values.shape[1:]
    seq_len = rows * ctx
    own_rows = filter_taps.shape[0]
    part = seq_len // dp
    pair = channels // WIDTH // (ctx // 4)
    outer = max(1, pair * OUTER_EIGHTHS // 8)
    inner = pair - outer
    most = max(outer, inner)
    forward, inverse = odd_tables(seq_len)
    half, full = jnp.bfloat16, jnp.float32
    whole = pltpu.VMEM((most, seq_len, WIDTH), half)
    halves = pltpu.VMEM((most, seq_len // 2, WIDTH), half)
    mix = pltpu.VMEM((2 * seq_len, WIDTH), half)
    block = pltpu.VMEM((rows, channels), half)
    pair_rows = pltpu.VMEM((2, rows, channels), half)
    sems = pltpu.SemaphoreType.DMA((2, most, ctx // 2))
    groups = pltpu.SemaphoreType.DMA((2, most, dp))
    anywhere = pl.BlockSpec(memory_space=pl.ANY)
    vmem = pl.BlockSpec(memory_space=pltpu.VMEM)
    shape = jax.ShapeDtypeStruct((rows, channels), half)
    flops = 12 * seq_len * seq_len * (channels // ctx) * 2
    output, gate_grad, values_grad, filter_grad = pl.pallas_call(
        functools.partial(kernel, (ctx, dp, rows, seq_len, outer, inner)),
        out_shape=(shape, shape, shape, jax.ShapeDtypeStruct((own_rows, channels), full)),
        in_specs=[anywhere] * 6,
        out_specs=(vmem,) * 4,
        scratch_shapes=[
            block, block, pltpu.VMEM((own_rows, channels), full),
            pltpu.VMEM(forward.shape, half), pltpu.VMEM(inverse.shape, half),
            pltpu.VMEM((own_rows, channels), half), pair_rows,
            halves, whole, whole, mix, mix, mix,
            halves, halves, whole, pltpu.VMEM((most, dp, part, WIDTH), half),
            pltpu.VMEM((most, part, WIDTH), half),
            pair_rows, pltpu.VMEM((2, own_rows, channels), half),
            pltpu.SemaphoreType.DMA((6,)), groups, groups,
        ] + [sems] * 9,
        compiler_params=pltpu.CompilerParams(
            collective_id=0, has_side_effects=True, vmem_limit_bytes=58 * 2**20
        ),
        cost_estimate=pl.CostEstimate(
            flops=flops, bytes_accessed=16 * rows * channels, transcendentals=0
        ),
    )(gate_input[0], values[0], cotangent[0], filter_taps, forward, inverse)
    return output[None], gate_grad[None], values_grad[None], filter_grad


def dft_tables(blocks, freq_len):
    half_blocks = blocks // 2
    row_index = jnp.arange(half_blocks, dtype=jnp.int32)[:, None]
    freq_index = jnp.arange(blocks, dtype=jnp.int32)[None, :]
    angles = (row_index * freq_index % blocks).astype(jnp.float32) * (2.0 * math.pi / blocks)
    first_forward = jnp.stack([jnp.cos(angles), -jnp.sin(angles)], axis=1).astype(jnp.bfloat16)
    first_inverse = jnp.stack([jnp.cos(angles).T, -jnp.sin(angles).T], axis=0).astype(jnp.bfloat16)
    block_index = jnp.arange(blocks, dtype=jnp.int32)[:, None]
    lane_index = jnp.arange(128, dtype=jnp.int32)[None, :]
    twist_angles = (block_index * lane_index % freq_len).astype(jnp.float32) * (
        2.0 * math.pi / freq_len
    )
    twist_cosine = jnp.cos(twist_angles)[:, :, None]
    twist_sine = jnp.sin(twist_angles)[:, :, None]
    inner_index = jnp.arange(128, dtype=jnp.int32)
    inner_angles = (inner_index[:, None] * inner_index[None, :] % 128).astype(jnp.float32) * (
        2.0 * math.pi / 128
    )
    cosine = jnp.cos(inner_angles)
    sine_part = jnp.sin(inner_angles)
    second_forward = jnp.stack(
        [jnp.stack([cosine, -sine_part], axis=1), jnp.stack([sine_part, cosine], axis=1)], axis=0
    ).astype(jnp.bfloat16)
    second_inverse = jnp.stack(
        [jnp.stack([cosine, sine_part], axis=1), jnp.stack([-sine_part, cosine], axis=1)], axis=0
    ).astype(jnp.bfloat16)
    return (first_forward, first_inverse, twist_cosine, twist_sine, second_forward, second_inverse)


def first_section(signal, matrix):
    grouped = signal.reshape(-1, 128, signal.shape[-1])
    return jnp.einsum("abc,arp->rpbc", grouped, matrix, preferred_element_type=jnp.float32)


def second_section(first, tables):
    twisted = jnp.stack(
        [first[0] * tables[2] + first[1] * tables[3], first[1] * tables[2] - first[0] * tables[3]]
    ).astype(jnp.bfloat16)
    return jnp.einsum("rpbc,rbsq->spqc", twisted, tables[4], preferred_element_type=jnp.float32)


def spectrum(signal, tables):
    return second_section(first_section(signal, tables[0]), tables)


def inverse_prepare(spectrum_half, tables):
    mixture = jnp.einsum(
        "rpqc,rqsb->spbc", spectrum_half, tables[5], preferred_element_type=jnp.float32
    )
    return jnp.stack(
        [
            mixture[0] * tables[2] - mixture[1] * tables[3],
            mixture[1] * tables[2] + mixture[0] * tables[3],
        ]
    ).astype(jnp.bfloat16)


def inverse_rows(twisted, matrix, norm_scale):
    rows = (
        jnp.einsum("rpbc,rpa->abc", twisted, matrix, preferred_element_type=jnp.float32)
        * norm_scale
    )
    return rows.reshape(-1, rows.shape[-1])


def times_spec(left_spec, right_spec):
    return jnp.stack(
        [
            left_spec[0] * right_spec[0] - left_spec[1] * right_spec[1],
            left_spec[0] * right_spec[1] + left_spec[1] * right_spec[0],
        ]
    ).astype(jnp.bfloat16)


def times_conj(left_spec, right_spec):
    return jnp.stack(
        [
            left_spec[0] * right_spec[0] + left_spec[1] * right_spec[1],
            left_spec[1] * right_spec[0] - left_spec[0] * right_spec[1],
        ]
    ).astype(jnp.bfloat16)


def multiply_round(left_side, right_side):
    return (left_side.astype(jnp.float32) * right_side.astype(jnp.float32)).astype(jnp.bfloat16)


def in_steps(gate_input, values, cotangent, filter_taps):
    context_size = lax.axis_size("ctx")
    data_size = lax.axis_size("dp")
    tok_rows = values.shape[1]
    channels = values.shape[2]
    seq_len = tok_rows * context_size
    local_channels = channels // context_size
    blocks = seq_len // 64
    freq_len = 2 * seq_len
    norm_scale = 1.0 / freq_len
    tables = dft_tables(blocks, freq_len)
    filter_half = filter_taps.astype(jnp.bfloat16)
    filter_columns = lax.all_to_all(filter_half, "ctx", split_axis=1, concat_axis=0, tiled=True)
    matrix = tables[0]
    filter_first = first_section(lax.all_gather(filter_columns, "dp", axis=0, tiled=True), matrix)
    filter_spec = second_section(filter_first, tables)
    value_columns = lax.all_to_all(values[0], "ctx", split_axis=1, concat_axis=0, tiled=True)
    value_spec = spectrum(value_columns, tables)
    conv_columns = inverse_rows(
        inverse_prepare(times_spec(value_spec, filter_spec), tables), tables[1], norm_scale
    ).astype(jnp.bfloat16)
    conv_rows = lax.all_to_all(conv_columns, "ctx", split_axis=0, concat_axis=1, tiled=True)
    output = multiply_round(gate_input[0], conv_rows)
    gate_grad = multiply_round(cotangent[0], conv_rows)
    grad_rows = multiply_round(cotangent[0], gate_input[0])
    grad_columns = lax.all_to_all(grad_rows, "ctx", split_axis=1, concat_axis=0, tiled=True)
    grad_spec = spectrum(grad_columns, tables)
    back_columns = inverse_rows(
        inverse_prepare(times_conj(grad_spec, filter_spec), tables), tables[1], norm_scale
    ).astype(jnp.bfloat16)
    values_grad = lax.all_to_all(back_columns, "ctx", split_axis=0, concat_axis=1, tiled=True)
    filter_twisted = inverse_prepare(times_conj(grad_spec, value_spec), tables)
    whole_rows = inverse_rows(filter_twisted, tables[1], norm_scale)
    reordered = whole_rows.reshape(data_size, context_size, tok_rows // data_size, local_channels)
    reordered = reordered.transpose(1, 0, 2, 3).reshape(seq_len, local_channels)
    received_rows = lax.all_to_all(
        reordered.astype(jnp.bfloat16), "ctx", split_axis=0, concat_axis=1, tiled=True
    ).astype(reordered.dtype)
    filter_grad = lax.psum_scatter(
        received_rows.astype(jnp.bfloat16), "dp", scatter_dimension=0, tiled=True
    ).astype(jnp.float32)
    return (output[None], gate_grad[None], values_grad[None], filter_grad)


def on_device(gate_input, values, cotangent, filter_taps):
    rows, channels = values.shape[1:]
    context_size = lax.axis_size("ctx")
    seq_len = rows * context_size
    table_bytes = 2 * 2 * 2 * seq_len * seq_len
    if table_bytes <= TABLE_LIMIT and context_size % 4 == 0 and channels % (WIDTH * context_size) == 0:
        return in_one_kernel(gate_input, values, cotangent, filter_taps)
    return in_steps(gate_input, values, cotangent, filter_taps)


def solution(mesh):
    in_specs = (
        P("dp", "ctx", None),
        P("dp", "ctx", None),
        P("dp", "ctx", None),
        P(("dp", "ctx"), None),
    )
    out_specs = (
        P("dp", "ctx", None),
        P("dp", "ctx", None),
        P("dp", "ctx", None),
        P(("dp", "ctx"), None),
    )
    return jax.shard_map(
        on_device, mesh=mesh, in_specs=in_specs, out_specs=out_specs, check_vma=False
    )
```

profile of v0, /device:TPU:0, one launch (start us, length us, event | category | flops | bytes accessed | tf_op | source)
XLA Modules:
  0.0 137.4 jit_solution(10704871212823204215)
XLA Ops:
  0.6 130.3 %shard_map.93 = (bf16[128,4096]{1,0:T(8,128)(2,1)}, bf16[128,4096]{1,0:T(8,128)(2,1)}, bf16[128,4096]{1,0:T(8,128)(2,1)}, f32[32,4096]{1,0:T(8,128)}) custom-call(bf16[128,4096]{1,0:T(8,128)(2,1)} %bitcast.9, bf16[128,4096]{1,0:T(8,128)(2,1)} %bitcast.10, bf16[128,4096]{1,0:T(8,128)(2,1)} %bitcast.11, f32[32,4096]{1,0:T(8,128)} %taps_hbm.1, ...), custom_call_target="tpu_custom_call" | custom-call | flops 12884901888 | bytes 8388608 | tf_op jit(solution)/shard_map/pallas_call | solution.py:409
  130.9 0.0 copy-start
  130.9 0.0 copy-start.1
  130.9 2.4 %copy.14 = bf16[1,128,4096]{2,1,0:T(8,128)(2,1)} copy(bf16[1,128,4096]{2,1,0:T(8,128)(2,1)} %bitcast.8) | data formatting | bytes 2097152
  133.3 2.3 %copy.15 = bf16[1,128,4096]{2,1,0:T(8,128)(2,1)} copy(bf16[1,128,4096]{2,1,0:T(8,128)(2,1)} %bitcast.7) | data formatting | bytes 2097152
  135.6 0.0 copy-done
  135.6 1.0 copy.16
  136.6 0.0 copy-done.1
  136.6 0.8 copy.17
Async XLA Ops:
  130.9 4.7 %copy-start = (bf16[128,4096]{1,0:T(8,128)(2,1)S(1)}, bf16[128,4096]{1,0:T(8,128)(2,1)}, u32[]{:S(2)}) copy-start(bf16[128,4096]{1,0:T(8,128)(2,1)} %get-tuple-element.10) | copy-start | bytes 3145732
  130.9 5.7 %copy-start.1 = (f32[32,4096]{1,0:T(8,128)S(1)}, f32[32,4096]{1,0:T(8,128)}, u32[]{:S(2)}) copy-start(f32[32,4096]{1,0:T(8,128)} %get-tuple-element.19) | copy-start | bytes 1572868
where the time goes:
time: 138 us; the launch traced here: 137 us
  Pallas kernels  130 us (94%)
  local copies, waits for them, and re-layouts  6.46 us (5%)
    pallas_call x1, Pallas kernels, in_one_kernel(): pl.pallas_call(functools.partial(kernel, (ctx, dp, rows, seq_len, outer,...  130 us
    unnamed x8, local copies, waits for them, and re-layouts  6.46 us

commit v1 on v0

--- a/solution.py
+++ b/solution.py
@@ -13,7 +13,7 @@
 WIDTH = 256
 TABLE_LIMIT = 8 * 2**20
 TILE = 256
-OUTER_EIGHTHS = 2
+OUTER_EIGHTHS = 4
 
 
 def odd_tables(seq_len):

time: 138 us -> 111 us (0.80)
  Pallas kernels: 130 us -> 104 us
    pallas_call x1, Pallas kernels: 130 us -> 104 us  [in_one_kernel(): pl.pallas_call(functools.partial(kernel, (ctx, dp, rows, seq_len, outer,...]
where the time goes in v1:
time: 111 us
  Pallas kernels  104 us (94%)
  local copies, waits for them, and re-layouts  6.46 us (6%)
    pallas_call x1, Pallas kernels, in_one_kernel(): pl.pallas_call(functools.partial(kernel, (ctx, dp, rows, seq_len, outer,...  104 us
    unnamed x8, local copies, waits for them, and re-layouts  6.46 us

profile of v1, /device:TPU:0, one launch (start us, length us, event | category | flops | bytes accessed | tf_op | source)
XLA Modules:
  0.0 110.9 jit_solution(8932963525002539984)
XLA Ops:
  0.6 103.7 %shard_map.93 = (bf16[128,4096]{1,0:T(8,128)(2,1)}, bf16[128,4096]{1,0:T(8,128)(2,1)}, bf16[128,4096]{1,0:T(8,128)(2,1)}, f32[32,4096]{1,0:T(8,128)}) custom-call(bf16[128,4096]{1,0:T(8,128)(2,1)} %bitcast.9, bf16[128,4096]{1,0:T(8,128)(2,1)} %bitcast.10, bf16[128,4096]{1,0:T(8,128)(2,1)} %bitcast.11, f32[32,4096]{1,0:T(8,128)} %taps_hbm.1, ...), custom_call_target="tpu_custom_call" | custom-call | flops 12884901888 | bytes 8388608 | tf_op jit(solution)/shard_map/pallas_call | solution.py:409
  104.4 0.0 copy-start
  104.4 0.0 copy-start.1
  104.4 2.4 %copy.14 = bf16[1,128,4096]{2,1,0:T(8,128)(2,1)} copy(bf16[1,128,4096]{2,1,0:T(8,128)(2,1)} %bitcast.8) | data formatting | bytes 2097152
  106.8 2.3 %copy.15 = bf16[1,128,4096]{2,1,0:T(8,128)(2,1)} copy(bf16[1,128,4096]{2,1,0:T(8,128)(2,1)} %bitcast.7) | data formatting | bytes 2097152
  109.1 0.0 copy-done
  109.1 1.0 copy.16
  110.1 0.0 copy-done.1
  110.1 0.8 copy.17
Async XLA Ops:
  104.4 4.7 %copy-start = (bf16[128,4096]{1,0:T(8,128)(2,1)S(1)}, bf16[128,4096]{1,0:T(8,128)(2,1)}, u32[]{:S(2)}) copy-start(bf16[128,4096]{1,0:T(8,128)(2,1)} %get-tuple-element.10) | copy-start | bytes 3145732
  104.4 5.7 %copy-start.1 = (f32[32,4096]{1,0:T(8,128)S(1)}, f32[32,4096]{1,0:T(8,128)}, u32[]{:S(2)}) copy-start(f32[32,4096]{1,0:T(8,128)} %get-tuple-element.19) | copy-start | bytes 1572868

commit v2 on v1

--- a/solution.py
+++ b/solution.py
@@ -12,7 +12,7 @@
 MESH = pl.DeviceIdType.MESH
 WIDTH = 256
 TABLE_LIMIT = 8 * 2**20
-TILE = 256
+TILE = 512
 OUTER_EIGHTHS = 4
 
 
@@ -21,7 +21,8 @@
     angles = turns * (2.0 * math.pi / (4 * seq_len))
     forward = np.concatenate([np.cos(angles), -np.sin(angles)], axis=0)
     inverse = forward.T / seq_len
-    forward = np.stack([forward[:, : seq_len // 2], forward[:, seq_len // 2 :]])
+    tiled = forward.reshape(2, seq_len // TILE, TILE, 2, seq_len // 2)
+    forward = tiled.transpose(3, 1, 0, 2, 4).reshape(2, 2 * seq_len, seq_len // 2)
     return jnp.asarray(forward, jnp.bfloat16), jnp.asarray(inverse, jnp.bfloat16)
 
 
@@ -40,7 +41,7 @@
 def kernel(
     dims,
     gate_hbm, values_hbm, cot_hbm, taps_hbm, forward_hbm, inverse_hbm,
-    out_ref, gate_grad_ref, values_grad_ref, filter_grad_ref,
+    result_rows_ref, filter_grad_ref,
     gate, cot, taps, forward, inverse, taps_half, signal_rows,
     near, whole, taps_cols, mixed_near, mixed_far, mixed_taps,
     near_cols, far_cols, partial, partial_in, summed, result_rows, summed_rows,
@@ -193,6 +194,13 @@
         barrier, inc=1, device_id={"dp": lax.rem(group + offset, dp)}, device_id_type=MESH))
     loads[0].wait()
     taps_half[...] = taps[...].astype(jnp.bfloat16)
+    pl.semaphore_wait(barrier, ctx + dp - 2)
+
+    def send_taps(chunk):
+        taps_cross_way.start(chunk)
+        taps_way.start(chunk)
+
+    loop(0, most, send_taps)
     loads[2].wait()
     loads[3].wait()
 
@@ -203,16 +211,13 @@
 
     loop(0, rows // 16, grad_band)
     loads[1].wait()
-    pl.semaphore_wait(barrier, ctx + dp - 2)
-
-    def send_in(chunk):
-        taps_cross_way.start(chunk)
-        taps_way.start(chunk)
+
+    def send_signals(chunk):
         cross_way.start(chunk)
         near_way.start(chunk)
         far_way.start(chunk)
 
-    loop(0, most, send_in)
+    send_signals(0)
     mine = count(me)
 
     def gathered(chunk, offset, owner):
@@ -227,6 +232,7 @@
         loop(1, dp, lambda offset: gathered(chunk, offset, group).start())
 
     loop(0, mine, gather)
+    loop(1, most, send_signals)
     loads[4].wait()
     loads[5].wait()
     sign = jnp.where(low, 1.0, -1.0).astype(jnp.float32)
@@ -273,16 +279,17 @@
         def frequencies(index):
             upper = block(index, TILE)
             lower = pl.ds(pl.multiple_of(seq_len + index * TILE, TILE), TILE)
-
-            def split(band):
-                taps_part = dot(forward[0, band, :], taps_cols[chunk, first, :]) + dot(
-                    forward[1, band, :], taps_cols[chunk, second, :])
-                near_part = dot(forward[half, band, :], near[chunk])
-                return (taps_part, near_part, dot(forward[0, band, :], whole[chunk, first, :]),
-                        dot(forward[1, band, :], whole[chunk, second, :]))
-
-            taps_real, near_real, early_real, late_real = split(upper)
-            taps_imag, near_imag, early_imag, late_imag = split(lower)
+            band = block(index, 2 * TILE)
+
+            def parts(both):
+                return both[:TILE], both[TILE:]
+
+            taps_real, taps_imag = parts(
+                dot(forward[0, band, :], taps_cols[chunk, first, :])
+                + dot(forward[1, band, :], taps_cols[chunk, second, :]))
+            near_real, near_imag = parts(dot(forward[half, band, :], near[chunk]))
+            early_real, early_imag = parts(dot(forward[0, band, :], whole[chunk, first, :]))
+            late_real, late_imag = parts(dot(forward[1, band, :], whole[chunk, second, :]))
             taps_imag = taps_imag * sign
             far_real, far_imag = early_real + late_real, early_imag + late_imag
             half_type = jnp.bfloat16
@@ -332,14 +339,7 @@
 
     loop(0, most, results)
 
-    def gate_band(index):
-        band = block(index, 16)
-        conv = result_rows[0, band, :].astype(jnp.float32)
-        out_ref[band, :] = (gate[band, :].astype(jnp.float32) * conv).astype(jnp.bfloat16)
-        gate_grad_ref[band, :] = (cot[band, :].astype(jnp.float32) * conv).astype(jnp.bfloat16)
-
-    loop(0, rows // 16, gate_band)
-    values_grad_ref[...] = result_rows[1]
+    result_rows_ref[...] = result_rows[...]
 
     @pl.when(low)
     def _():
@@ -380,6 +380,32 @@
             summed_way.leave(chunk)
 
     loop(0, mine, sent_sums)
+
+
+def gate_kernel(gate, cot, rows, sums, out_ref, gate_grad_ref, values_grad_ref, filter_grad_ref):
+    conv = rows[0].astype(jnp.float32)
+    out_ref[...] = (gate[...].astype(jnp.float32) * conv).astype(jnp.bfloat16)
+    gate_grad_ref[...] = (cot[...].astype(jnp.float32) * conv).astype(jnp.bfloat16)
+    values_grad_ref[...] = rows[1]
+    filter_grad_ref[...] = sums[...]
+
+
+def gate_results(gate_input, cotangent, result_rows, sums):
+    rows, channels = gate_input.shape
+    own_rows = sums.shape[0]
+    steps = own_rows // 8
+    block = pl.BlockSpec((rows // steps, channels), lambda i: (i, 0))
+    pair = pl.BlockSpec((2, rows // steps, channels), lambda i: (0, i, 0))
+    few = pl.BlockSpec((8, channels), lambda i: (i, 0))
+    shape = jax.ShapeDtypeStruct((rows, channels), jnp.bfloat16)
+    return pl.pallas_call(
+        gate_kernel,
+        grid=(steps,),
+        in_specs=[block, block, pair, few],
+        out_specs=(block, block, block, few),
+        out_shape=(shape, shape, shape, jax.ShapeDtypeStruct(sums.shape, jnp.float32)),
+        compiler_params=pltpu.CompilerParams(vmem_limit_bytes=24 * 2**20),
+    )(gate_input, cotangent, result_rows, sums)
 
 
 def in_one_kernel(gate_input, values, cotangent, filter_taps):
@@ -404,13 +430,15 @@
     groups = pltpu.SemaphoreType.DMA((2, most, dp))
     anywhere = pl.BlockSpec(memory_space=pl.ANY)
     vmem = pl.BlockSpec(memory_space=pltpu.VMEM)
-    shape = jax.ShapeDtypeStruct((rows, channels), half)
     flops = 12 * seq_len * seq_len * (channels // ctx) * 2
-    output, gate_grad, values_grad, filter_grad = pl.pallas_call(
+    result_rows, sums = pl.pallas_call(
         functools.partial(kernel, (ctx, dp, rows, seq_len, outer, inner)),
-        out_shape=(shape, shape, shape, jax.ShapeDtypeStruct((own_rows, channels), full)),
+        out_shape=(
+            jax.ShapeDtypeStruct((2, rows, channels), half),
+            jax.ShapeDtypeStruct((own_rows, channels), full),
+        ),
         in_specs=[anywhere] * 6,
-        out_specs=(vmem,) * 4,
+        out_specs=(vmem,) * 2,
         scratch_shapes=[
             block, block, pltpu.VMEM((own_rows, channels), full),
             pltpu.VMEM(forward.shape, half), pltpu.VMEM(inverse.shape, half),
@@ -428,6 +456,9 @@
             flops=flops, bytes_accessed=16 * rows * channels, transcendentals=0
         ),
     )(gate_input[0], values[0], cotangent[0], filter_taps, forward, inverse)
+    output, gate_grad, values_grad, filter_grad = gate_results(
+        gate_input[0], cotangent[0], result_rows, sums
+    )
     return output[None], gate_grad[None], values_grad[None], filter_grad
 
 

time: 111 us -> 104 us (0.937)
  local copies, waits for them, and re-layouts: 6.46 us -> 2.63 us
  Pallas kernels: 104 us -> 101 us
    pallas_call x1, Pallas kernels: 104 us -> 98.2 us  [in_one_kernel(): pl.pallas_call(functools.partial(kernel, (ctx, dp, rows, seq_len, outer,...]
    unnamed x8, local copies, waits for them, and re-layouts: 6.46 us -> 2.63 us
    pallas_call x0 -> x1, Pallas kernels: none -> 2.41 us  [gate_results(): pl.pallas_call(gate_kernel, grid=(steps,), in_specs=[block, block, pair,...]
where the time goes in v2:
time: 104 us
  Pallas kernels  101 us (97%)
  local copies, waits for them, and re-layouts  2.63 us (3%)
    pallas_call x1, Pallas kernels, in_one_kernel(): pl.pallas_call(functools.partial(kernel, (ctx, dp, rows, seq_len, outer,...  98.2 us
    unnamed x8, local copies, waits for them, and re-layouts  2.63 us
    pallas_call x1, Pallas kernels, gate_results(): pl.pallas_call(gate_kernel, grid=(steps,), in_specs=[block, block, pair,...  2.41 us

profile of v2, /device:TPU:0, one launch (start us, length us, event | category | flops | bytes accessed | tf_op | source)
XLA Modules:
  0.0 103.9 jit_solution(13464671776622584737)
XLA Ops:
  0.6 0.0 copy-start.1
  0.6 0.0 copy-start.2
  0.7 98.2 %shard_map.93 = (bf16[2,128,4096]{2,1,0:T(8,128)(2,1)}, f32[32,4096]{1,0:T(8,128)}) custom-call(bf16[128,4096]{1,0:T(8,128)(2,1)} %bitcast.6, bf16[128,4096]{1,0:T(8,128)(2,1)} %bitcast.10, bf16[128,4096]{1,0:T(8,128)(2,1)} %bitcast.8, f32[32,4096]{1,0:T(8,128)} %taps_hbm.1, bf16[2,2048,512]{2,1,0:T(8,128)(2,1)} %constant.4.clone.forward_hbm, ...), custom_call_target="tpu_custom_call" | custom-call | flops 12884901888 | bytes 8388608 | tf_op jit(solution)/shard_map/pallas_call | solution.py:434
  98.9 0.0 copy-done.1
  98.9 0.0 copy-done.2
  98.9 0.0 copy-start
  98.9 1.6 %copy-done = bf16[2,128,4096]{2,1,0:T(8,128)(2,1)S(1)} copy-done((bf16[2,128,4096]{2,1,0:T(8,128)(2,1)S(1)}, bf16[2,128,4096]{2,1,0:T(8,128)(2,1)}, u32[]{:S(2)}) %copy-start) | copy-done | bytes 2097176
  100.5 0.0 copy-start.3
  100.5 1.0 %copy-done.3 = f32[32,4096]{1,0:T(8,128)S(1)} copy-done((f32[32,4096]{1,0:T(8,128)S(1)}, f32[32,4096]{1,0:T(8,128)}, u32[]{:S(2)}) %copy-start.3) | copy-done | bytes 524312
  101.5 2.4 %shard_map.94 = (bf16[128,4096]{1,0:T(8,128)(2,1)}, bf16[128,4096]{1,0:T(8,128)(2,1)}, bf16[128,4096]{1,0:T(8,128)(2,1)}, f32[32,4096]{1,0:T(8,128)}) custom-call(bf16[128,4096]{1,0:T(8,128)(2,1)S(1)} %bitcast.7, bf16[128,4096]{1,0:T(8,128)(2,1)S(1)} %bitcast.9, bf16[2,128,4096]{2,1,0:T(8,128)(2,1)S(1)} %copy-done, f32[32,4096]{1,0:T(8,128)S(1)} %copy-done.3), custom_call_target="tpu_custom_call" | custom-call | tf_op jit(solution)/shard_map/pallas_call | solution.py:401
Async XLA Ops:
  0.6 98.2 %copy-start.1 = (bf16[1,128,4096]{2,1,0:T(8,128)(2,1)S(1)}, bf16[1,128,4096]{2,1,0:T(8,128)(2,1)}, u32[]{:S(2)}) copy-start(bf16[1,128,4096]{2,1,0:T(8,128)(2,1)} %param.6) | copy-start | bytes 3145732
  0.6 98.2 %copy-start.2 = (bf16[1,128,4096]{2,1,0:T(8,128)(2,1)S(1)}, bf16[1,128,4096]{2,1,0:T(8,128)(2,1)}, u32[]{:S(2)}) copy-start(bf16[1,128,4096]{2,1,0:T(8,128)(2,1)} %param.8) | copy-start | bytes 3145732
  98.9 1.6 %copy-start = (bf16[2,128,4096]{2,1,0:T(8,128)(2,1)S(1)}, bf16[2,128,4096]{2,1,0:T(8,128)(2,1)}, u32[]{:S(2)}) copy-start(bf16[2,128,4096]{2,1,0:T(8,128)(2,1)} %get-tuple-element.10.rows) | copy-start | bytes 6291460
  100.5 1.0 %copy-start.3 = (f32[32,4096]{1,0:T(8,128)S(1)}, f32[32,4096]{1,0:T(8,128)}, u32[]{:S(2)}) copy-start(f32[32,4096]{1,0:T(8,128)} %get-tuple-element.11.sums) | copy-start | bytes 1572868

commit v3 on v2

--- a/solution.py
+++ b/solution.py
@@ -43,7 +43,7 @@
     gate_hbm, values_hbm, cot_hbm, taps_hbm, forward_hbm, inverse_hbm,
     result_rows_ref, filter_grad_ref,
     gate, cot, taps, forward, inverse, taps_half, signal_rows,
-    near, whole, taps_cols, mixed_near, mixed_far, mixed_taps,
+    near, whole, taps_cols, taps_spec, near_spec, mixed_near, mixed_far, mixed_taps,
     near_cols, far_cols, partial, partial_in, summed, result_rows, summed_rows,
     load_sem, gather_sem, reduce_sem,
     near_sem, cross_sem, far_sem, taps_sem, taps_cross_sem, back_near_sem, back_far_sem,
@@ -180,11 +180,11 @@
     loads = [
         pltpu.make_async_copy(src, dst, load_sem.at[at])
         for at, (src, dst) in enumerate(
-            [(taps_hbm, taps), (values_hbm, signal_rows.at[half]), (gate_hbm, gate),
-             (cot_hbm, cot), (forward_hbm, forward), (inverse_hbm, inverse)]
+            [(taps_hbm, taps), (gate_hbm, gate), (cot_hbm, cot),
+             (values_hbm, signal_rows.at[half]), (forward_hbm, forward), (inverse_hbm, inverse)]
         )
     ]
-    for load in loads:
+    for load in loads[:4]:
         load.start()
 
     barrier = pltpu.get_barrier_semaphore()
@@ -201,8 +201,8 @@
         taps_way.start(chunk)
 
     loop(0, most, send_taps)
+    loads[1].wait()
     loads[2].wait()
-    loads[3].wait()
 
     def grad_band(index):
         band = block(index, 16)
@@ -210,14 +210,16 @@
         signal_rows[1 - half, band, :] = product.astype(jnp.bfloat16)
 
     loop(0, rows // 16, grad_band)
-    loads[1].wait()
+    loads[3].wait()
 
     def send_signals(chunk):
+        near_way.start(chunk)
         cross_way.start(chunk)
-        near_way.start(chunk)
         far_way.start(chunk)
 
     send_signals(0)
+    loads[4].start()
+    loads[5].start()
     mine = count(me)
 
     def gathered(chunk, offset, owner):
@@ -269,66 +271,84 @@
             summed_way.start(chunk)
 
     def work(chunk):
-        cross_way.arrive(chunk)
-        near_way.arrive(chunk)
-        far_way.arrive(chunk)
         loop(1, dp, lambda offset: gathered(
             chunk, offset, lax.rem(group + dp - offset, dp)).wait_recv())
         first, second = pl.ds(0, half_len), pl.ds(half_len, half_len)
-
-        def frequencies(index):
+        half_type = jnp.bfloat16
+
+        def places(index):
             upper = block(index, TILE)
             lower = pl.ds(pl.multiple_of(seq_len + index * TILE, TILE), TILE)
-            band = block(index, 2 * TILE)
-
-            def parts(both):
-                return both[:TILE], both[TILE:]
-
-            taps_real, taps_imag = parts(
-                dot(forward[0, band, :], taps_cols[chunk, first, :])
-                + dot(forward[1, band, :], taps_cols[chunk, second, :]))
-            near_real, near_imag = parts(dot(forward[half, band, :], near[chunk]))
+            return upper, lower, block(index, 2 * TILE)
+
+        def parts(both):
+            return both[:TILE], both[TILE:]
+
+        def taps_frequencies(index):
+            band = places(index)[2]
+            taps_spec[band, :] = dot(forward[0, band, :], taps_cols[chunk, first, :]) + dot(
+                forward[1, band, :], taps_cols[chunk, second, :])
+
+        loop(0, seq_len // TILE, taps_frequencies)
+        near_way.arrive(chunk)
+
+        def near_frequencies(index):
+            upper, lower, band = places(index)
+            both = dot(forward[half, band, :], near[chunk])
+            near_spec[band, :] = both
+            near_real, near_imag = parts(both)
+            taps_real, taps_imag = parts(taps_spec[band, :])
+            taps_imag = taps_imag * sign
+            mixed_near[upper, :] = (near_real * taps_real - near_imag * taps_imag).astype(half_type)
+            mixed_near[lower, :] = (near_real * taps_imag + near_imag * taps_real).astype(half_type)
+
+        loop(0, seq_len // TILE, near_frequencies)
+
+        def inverse_rows(index):
+            return inverse[pl.ds(pl.multiple_of(half * half_len + index * TILE, TILE), TILE), :]
+
+        def near_tile(index):
+            near_cols[chunk, block(index, TILE), :] = dot(
+                inverse_rows(index), mixed_near[...]).astype(half_type)
+
+        def far_tile(index):
+            far_cols[chunk, block(index, TILE), :] = dot(
+                inverse_rows(index), mixed_far[...]).astype(half_type)
+
+        def taps_tile(index):
+            band = block(index, TILE)
+            partial[chunk, band, :] = dot(inverse[band, :], mixed_taps[...]).astype(half_type)
+
+        loop(0, half_len // TILE, near_tile)
+        back_near_way.start(chunk)
+        cross_way.arrive(chunk)
+        far_way.arrive(chunk)
+
+        def far_frequencies(index):
+            upper, lower, band = places(index)
             early_real, early_imag = parts(dot(forward[0, band, :], whole[chunk, first, :]))
             late_real, late_imag = parts(dot(forward[1, band, :], whole[chunk, second, :]))
-            taps_imag = taps_imag * sign
-            far_real, far_imag = early_real + late_real, early_imag + late_imag
-            half_type = jnp.bfloat16
-            mixed_near[upper, :] = (near_real * taps_real - near_imag * taps_imag).astype(half_type)
-            mixed_near[lower, :] = (near_real * taps_imag + near_imag * taps_real).astype(half_type)
-            mixed_far[upper, :] = (far_real * taps_real + far_imag * taps_imag).astype(half_type)
-            mixed_far[lower, :] = (far_imag * taps_real - far_real * taps_imag).astype(half_type)
+            near_real, near_imag = parts(near_spec[band, :])
             part_real, part_imag = early_real * keep + late_real, early_imag * keep + late_imag
             mixed_taps[upper, :] = (part_real * near_real + part_imag * near_imag).astype(half_type)
             mixed_taps[lower, :] = (
                 (part_imag * near_real - part_real * near_imag) * sign).astype(half_type)
-
-        loop(0, seq_len // TILE, frequencies)
-
-        def inverse_rows(index):
-            return inverse[pl.ds(pl.multiple_of(half * half_len + index * TILE, TILE), TILE), :]
-
-        def near_tile(index):
-            near_cols[chunk, block(index, TILE), :] = dot(
-                inverse_rows(index), mixed_near[...]).astype(jnp.bfloat16)
-
-        def far_tile(index):
-            far_cols[chunk, block(index, TILE), :] = dot(
-                inverse_rows(index), mixed_far[...]).astype(jnp.bfloat16)
-
-        def taps_tile(index):
-            band = block(index, TILE)
-            partial[chunk, band, :] = dot(inverse[band, :], mixed_taps[...]).astype(jnp.bfloat16)
-
-        loop(0, half_len // TILE, near_tile)
-        back_near_way.start(chunk)
+            far_real, far_imag = early_real + late_real, early_imag + late_imag
+            taps_real, taps_imag = parts(taps_spec[band, :])
+            taps_imag = taps_imag * sign
+            mixed_far[upper, :] = (far_real * taps_real + far_imag * taps_imag).astype(half_type)
+            mixed_far[lower, :] = (far_imag * taps_real - far_real * taps_imag).astype(half_type)
+
+        loop(0, seq_len // TILE, far_frequencies)
         loop(0, (2 - half) * (half_len // TILE), taps_tile)
         reduce_each(chunk, lambda copy: copy.start())
-        loop(0, half_len // TILE, far_tile)
-        back_far_way.start(chunk)
 
         @pl.when(chunk > 0)
         def _():
             finish(chunk - 1)
+
+        loop(0, half_len // TILE, far_tile)
+        back_far_way.start(chunk)
 
     loop(0, mine, work)
     finish(mine - 1)
@@ -404,7 +424,7 @@
         in_specs=[block, block, pair, few],
         out_specs=(block, block, block, few),
         out_shape=(shape, shape, shape, jax.ShapeDtypeStruct(sums.shape, jnp.float32)),
-        compiler_params=pltpu.CompilerParams(vmem_limit_bytes=24 * 2**20),
+        compiler_params=pltpu.CompilerParams(vmem_limit_bytes=60 * 2**20),
     )(gate_input, cotangent, result_rows, sums)
 
 
@@ -424,6 +444,7 @@
     whole = pltpu.VMEM((most, seq_len, WIDTH), half)
     halves = pltpu.VMEM((most, seq_len // 2, WIDTH), half)
     mix = pltpu.VMEM((2 * seq_len, WIDTH), half)
+    spec = pltpu.VMEM((2 * seq_len, WIDTH), full)
     block = pltpu.VMEM((rows, channels), half)
     pair_rows = pltpu.VMEM((2, rows, channels), half)
     sems = pltpu.SemaphoreType.DMA((2, most, ctx // 2))
@@ -443,7 +464,7 @@
             block, block, pltpu.VMEM((own_rows, channels), full),
             pltpu.VMEM(forward.shape, half), pltpu.VMEM(inverse.shape, half),
             pltpu.VMEM((own_rows, channels), half), pair_rows,
-            halves, whole, whole, mix, mix, mix,
+            halves, whole, whole, spec, spec, mix, mix, mix,
             halves, halves, whole, pltpu.VMEM((most, dp, part, WIDTH), half),
             pltpu.VMEM((most, part, WIDTH), half),
             pair_rows, pltpu.VMEM((2, own_rows, channels), half),

time: 104 us -> 104 us (level)
  local copies, waits for them, and re-layouts: 2.63 us -> 0 us
  Pallas kernels: 101 us -> 103 us
    unnamed x8 -> x0, local copies, waits for them, and re-layouts: 2.63 us -> none
    pallas_call x1, Pallas kernels: 2.41 us -> 4.59 us  [gate_results(): pl.pallas_call(gate_kernel, grid=(steps,), in_specs=[block, block, pair,...]
where the time goes in v3:
time: 104 us; the launch traced here: 103 us
  Pallas kernels  103 us (99%)
    pallas_call x1, Pallas kernels, in_one_kernel(): pl.pallas_call(functools.partial(kernel, (ctx, dp, rows, seq_len, outer,...  98.2 us
    pallas_call x1, Pallas kernels, gate_results(): pl.pallas_call(gate_kernel, grid=(steps,), in_specs=[block, block, pair,...  4.59 us

profile of v3, /device:TPU:0, one launch (start us, length us, event | category | flops | bytes accessed | tf_op | source)
XLA Modules:
  0.0 103.4 jit_solution(4197125188972474929)
XLA Ops:
  0.6 98.2 %shard_map.93 = (bf16[2,128,4096]{2,1,0:T(8,128)(2,1)}, f32[32,4096]{1,0:T(8,128)}) custom-call(bf16[128,4096]{1,0:T(8,128)(2,1)} %bitcast.6, bf16[128,4096]{1,0:T(8,128)(2,1)} %bitcast.10, bf16[128,4096]{1,0:T(8,128)(2,1)} %bitcast.8, f32[32,4096]{1,0:T(8,128)} %taps_hbm.1, bf16[2,2048,512]{2,1,0:T(8,128)(2,1)} %constant.4.clone.forward_hbm, ...), custom_call_target="tpu_custom_call" | custom-call | flops 12884901888 | bytes 8388608 | tf_op jit(solution)/shard_map/pallas_call | solution.py:455
  98.9 4.6 %shard_map.94 = (bf16[128,4096]{1,0:T(8,128)(2,1)}, bf16[128,4096]{1,0:T(8,128)(2,1)}, bf16[128,4096]{1,0:T(8,128)(2,1)}, f32[32,4096]{1,0:T(8,128)}) custom-call(bf16[128,4096]{1,0:T(8,128)(2,1)} %bitcast.7, bf16[128,4096]{1,0:T(8,128)(2,1)} %bitcast.9, bf16[2,128,4096]{2,1,0:T(8,128)(2,1)} %get-tuple-element.10.rows, f32[32,4096]{1,0:T(8,128)} %get-tuple-element.11.sums), custom_call_target="tpu_custom_call" | custom-call | tf_op jit(solution)/shard_map/pallas_call | solution.py:421

commit v4 on v3

--- a/solution.py
+++ b/solution.py
@@ -12,18 +12,34 @@
 MESH = pl.DeviceIdType.MESH
 WIDTH = 256
 TABLE_LIMIT = 8 * 2**20
-TILE = 512
 OUTER_EIGHTHS = 4
 
 
 def odd_tables(seq_len):
-    turns = np.outer(2 * np.arange(seq_len) + 1, np.arange(seq_len)) % (4 * seq_len)
-    angles = turns * (2.0 * math.pi / (4 * seq_len))
+    half_len = seq_len // 2
+    turns = np.outer(2 * np.arange(half_len) + 1, np.arange(half_len)) % (2 * seq_len)
+    angles = turns * (math.pi / seq_len)
     forward = np.concatenate([np.cos(angles), -np.sin(angles)], axis=0)
     inverse = forward.T / seq_len
-    tiled = forward.reshape(2, seq_len // TILE, TILE, 2, seq_len // 2)
-    forward = tiled.transpose(3, 1, 0, 2, 4).reshape(2, 2 * seq_len, seq_len // 2)
-    return jnp.asarray(forward, jnp.bfloat16), jnp.asarray(inverse, jnp.bfloat16)
+    forward = np.stack([forward[:, : half_len // 2], forward[:, half_len // 2 :]])
+    steps = (2 * np.arange(half_len) + 1)[:, None] * (math.pi / (2 * seq_len)) * np.ones((1, WIDTH))
+    twist = np.stack([np.cos(steps), np.sin(steps)])
+    return (jnp.asarray(forward, jnp.bfloat16), jnp.asarray(inverse, jnp.bfloat16),
+            jnp.asarray(twist, jnp.float32))
+
+
+def parting(rows):
+    row = lax.broadcasted_iota(jnp.int32, (rows, rows), 0)
+    column = lax.broadcasted_iota(jnp.int32, (rows, rows), 1)
+    source = jnp.where(row < rows // 2, 2 * row, 2 * row + 1 - rows)
+    return jnp.where(column == source, 1.0, 0.0).astype(jnp.bfloat16)
+
+
+def joining(rows):
+    row = lax.broadcasted_iota(jnp.int32, (rows, rows), 0)
+    column = lax.broadcasted_iota(jnp.int32, (rows, rows), 1)
+    source = jnp.where(column < rows // 2, 2 * column, 2 * column + 1 - rows)
+    return jnp.where(row == source, 1.0, 0.0).astype(jnp.bfloat16)
 
 
 def dot(left, right):
@@ -40,9 +56,9 @@
 
 def kernel(
     dims,
-    gate_hbm, values_hbm, cot_hbm, taps_hbm, forward_hbm, inverse_hbm,
-    result_rows_ref, filter_grad_ref,
-    gate, cot, taps, forward, inverse, taps_half, signal_rows,
+    gate_hbm, values_hbm, cot_hbm, taps_hbm, forward_hbm, inverse_hbm, twist_hbm,
+    result_rows_ref, sums_ref,
+    gate, cot, values, taps, forward, inverse, twist, taps_half, signal_rows,
     near, whole, taps_cols, taps_spec, near_spec, mixed_near, mixed_far, mixed_taps,
     near_cols, far_cols, partial, partial_in, summed, result_rows, summed_rows,
     load_sem, gather_sem, reduce_sem,
@@ -140,32 +156,32 @@
             self.each(chunk, True, lambda offset: self.to(chunk, offset).wait_send())
 
     def near_refs(chunk, sender, receiver):
-        return (signal_rows.at[0, :, columns(receiver, chunk)],
-                near.at[chunk, block(lax.rem(sender, side), rows), :])
+        return (signal_rows.at[0, :, :, columns(receiver, chunk)],
+                near.at[chunk, :, block(lax.rem(sender, side), rows // 2), :])
 
     def cross_refs(chunk, sender, receiver):
-        return (signal_rows.at[0, :, columns(receiver, chunk)],
-                whole.at[chunk, block(sender, rows), :])
+        return (signal_rows.at[0, :, :, columns(receiver, chunk)],
+                whole.at[chunk, :, block(sender, rows // 2), :])
 
     def far_refs(chunk, sender, receiver):
-        return (signal_rows.at[1, :, columns(receiver, chunk)],
-                whole.at[chunk, block(sender, rows), :])
+        return (signal_rows.at[1, :, :, columns(receiver, chunk)],
+                whole.at[chunk, :, block(sender, rows // 2), :])
 
     def taps_refs(chunk, sender, receiver):
-        return (taps_half.at[:, columns(receiver, chunk)],
-                taps_cols.at[chunk, block(group * ctx + sender, own_rows), :])
+        return (taps_half.at[:, :, columns(receiver, chunk)],
+                taps_cols.at[chunk, :, block(group * ctx + sender, own_rows // 2), :])
 
     def back_near_refs(chunk, sender, receiver):
-        return (near_cols.at[chunk, block(lax.rem(receiver, side), rows), :],
-                result_rows.at[half, :, columns(sender, chunk)])
+        return (near_cols.at[chunk, :, block(lax.rem(receiver, side), rows // 2), :],
+                result_rows.at[half, :, :, columns(sender, chunk)])
 
     def back_far_refs(chunk, sender, receiver):
-        return (far_cols.at[chunk, block(lax.rem(receiver, side), rows), :],
-                result_rows.at[1 - half, :, columns(sender, chunk)])
+        return (far_cols.at[chunk, :, block(lax.rem(receiver, side), rows // 2), :],
+                result_rows.at[1 - half, :, :, columns(sender, chunk)])
 
     def summed_refs(chunk, sender, receiver):
-        return (summed.at[chunk, block(receiver, own_rows), :],
-                summed_rows.at[sender // side, :, columns(sender, chunk)])
+        return (summed.at[chunk, :, block(receiver, own_rows // 2), :],
+                summed_rows.at[sender // side, :, :, columns(sender, chunk)])
 
     near_way = Exchange(near_refs, near_sem, False, True)
     cross_way = Exchange(cross_refs, cross_sem, True, True)
@@ -181,7 +197,8 @@
         pltpu.make_async_copy(src, dst, load_sem.at[at])
         for at, (src, dst) in enumerate(
             [(taps_hbm, taps), (gate_hbm, gate), (cot_hbm, cot),
-             (values_hbm, signal_rows.at[half]), (forward_hbm, forward), (inverse_hbm, inverse)]
+             (values_hbm, values), (forward_hbm, forward), (inverse_hbm, inverse),
+             (twist_hbm, twist)]
         )
     ]
     for load in loads[:4]:
@@ -193,7 +210,19 @@
     loop(1, dp, lambda offset: pl.semaphore_signal(
         barrier, inc=1, device_id={"dp": lax.rem(group + offset, dp)}, device_id_type=MESH))
     loads[0].wait()
-    taps_half[...] = taps[...].astype(jnp.bfloat16)
+
+    def apart(target, source, order):
+        both = dot(order, source).astype(jnp.bfloat16)
+        target[0], target[1] = both[: both.shape[0] // 2], both[both.shape[0] // 2 :]
+
+    channels = gate.shape[1]
+    span = 512
+
+    def taps_band(index):
+        band = block(index, span)
+        apart(taps_half.at[:, :, band], taps[:, band].astype(jnp.bfloat16), parting(own_rows))
+
+    loop(0, channels // span, taps_band)
     pl.semaphore_wait(barrier, ctx + dp - 2)
 
     def send_taps(chunk):
@@ -205,12 +234,18 @@
     loads[2].wait()
 
     def grad_band(index):
-        band = block(index, 16)
-        product = gate[band, :].astype(jnp.float32) * cot[band, :].astype(jnp.float32)
-        signal_rows[1 - half, band, :] = product.astype(jnp.bfloat16)
-
-    loop(0, rows // 16, grad_band)
+        band = block(index, span)
+        product = gate[:, band].astype(jnp.float32) * cot[:, band].astype(jnp.float32)
+        apart(signal_rows.at[1 - half, :, :, band], product.astype(jnp.bfloat16), parting(rows))
+
+    loop(0, channels // span, grad_band)
     loads[3].wait()
+
+    def value_band(index):
+        band = block(index, span)
+        apart(signal_rows.at[half, :, :, band], values[:, band], parting(rows))
+
+    loop(0, channels // span, value_band)
 
     def send_signals(chunk):
         near_way.start(chunk)
@@ -220,11 +255,12 @@
     send_signals(0)
     loads[4].start()
     loads[5].start()
+    loads[6].start()
     mine = count(me)
 
     def gathered(chunk, offset, owner):
         peer = lax.rem(group + offset, dp)
-        held = taps_cols.at[chunk, block(owner, part), :]
+        held = taps_cols.at[chunk, :, block(owner, part // 2), :]
         return remote(held, held, gather_sem.at[0, chunk, offset], gather_sem.at[1, chunk, offset],
                       {"dp": peer})
 
@@ -237,6 +273,7 @@
     loop(1, most, send_signals)
     loads[4].wait()
     loads[5].wait()
+    loads[6].wait()
     sign = jnp.where(low, 1.0, -1.0).astype(jnp.float32)
     keep = jnp.where(low, 1.0, 0.0).astype(jnp.float32)
 
@@ -245,7 +282,7 @@
 
     def reduced(chunk, offset, owner):
         return remote(
-            partial.at[chunk, block(owner, part), :], partial_in.at[chunk, offset],
+            partial.at[chunk, :, block(owner, part // 2), :], partial_in.at[chunk, offset],
             reduce_sem.at[0, chunk, offset], reduce_sem.at[1, chunk, offset],
             {"dp": lax.rem(group + offset, dp)})
 
@@ -263,7 +300,7 @@
         @pl.when(reduces(group))
         def _():
             loop(1, dp, lambda offset: reduced(chunk, offset, group).wait_recv())
-            total = partial[chunk, block(group, part), :].astype(jnp.float32)
+            total = partial[chunk, :, block(group, part // 2), :].astype(jnp.float32)
             for offset in range(1, dp):
                 total = total + partial_in[chunk, offset].astype(jnp.float32)
             summed[chunk] = total.astype(jnp.bfloat16)
@@ -273,81 +310,82 @@
     def work(chunk):
         loop(1, dp, lambda offset: gathered(
             chunk, offset, lax.rem(group + dp - offset, dp)).wait_recv())
-        first, second = pl.ds(0, half_len), pl.ds(half_len, half_len)
-        half_type = jnp.bfloat16
-
-        def places(index):
-            upper = block(index, TILE)
-            lower = pl.ds(pl.multiple_of(seq_len + index * TILE, TILE), TILE)
-            return upper, lower, block(index, 2 * TILE)
+        quarter = half_len // 2
+        first, second = pl.ds(0, quarter), pl.ds(quarter, quarter)
 
         def parts(both):
-            return both[:TILE], both[TILE:]
-
-        def taps_frequencies(index):
-            band = places(index)[2]
-            taps_spec[band, :] = dot(forward[0, band, :], taps_cols[chunk, first, :]) + dot(
-                forward[1, band, :], taps_cols[chunk, second, :])
-
-        loop(0, seq_len // TILE, taps_frequencies)
+            return both[:half_len], both[half_len:]
+
+        def turned(odd):
+            real, imag = parts(odd)
+            return twist[0] * real + twist[1] * imag, twist[0] * imag - twist[1] * real
+
+        def butterfly(even, odd):
+            real, imag = parts(even)
+            turned_real, turned_imag = turned(odd)
+            return (real + turned_real, imag + turned_imag, real - turned_real, imag - turned_imag)
+
+        def unmix(target, real, imag, mirror_real, mirror_imag):
+            target[0, :half_len, :] = (real + mirror_real).astype(jnp.bfloat16)
+            target[0, half_len:, :] = (imag + mirror_imag).astype(jnp.bfloat16)
+            real, imag = real - mirror_real, imag - mirror_imag
+            target[1, :half_len, :] = (twist[0] * real - twist[1] * imag).astype(jnp.bfloat16)
+            target[1, half_len:, :] = (twist[0] * imag + twist[1] * real).astype(jnp.bfloat16)
+
+        def times(left, right):
+            return left[0] * right[0] - left[1] * right[1], left[0] * right[1] + left[1] * right[0]
+
+        def times_conjugate(left, right):
+            return left[0] * right[0] + left[1] * right[1], left[1] * right[0] - left[0] * right[1]
+
+        def of_taps(parity):
+            return dot(forward[0], taps_cols[chunk, parity, first, :]) + dot(
+                forward[1], taps_cols[chunk, parity, second, :])
+
+        spectrum = butterfly(of_taps(0), of_taps(1))
+        taps_spec[0], taps_spec[1] = spectrum[0], spectrum[1] * sign
+        taps_spec[2], taps_spec[3] = spectrum[2], spectrum[3] * sign
         near_way.arrive(chunk)
-
-        def near_frequencies(index):
-            upper, lower, band = places(index)
-            both = dot(forward[half, band, :], near[chunk])
-            near_spec[band, :] = both
-            near_real, near_imag = parts(both)
-            taps_real, taps_imag = parts(taps_spec[band, :])
-            taps_imag = taps_imag * sign
-            mixed_near[upper, :] = (near_real * taps_real - near_imag * taps_imag).astype(half_type)
-            mixed_near[lower, :] = (near_real * taps_imag + near_imag * taps_real).astype(half_type)
-
-        loop(0, seq_len // TILE, near_frequencies)
-
-        def inverse_rows(index):
-            return inverse[pl.ds(pl.multiple_of(half * half_len + index * TILE, TILE), TILE), :]
-
-        def near_tile(index):
-            near_cols[chunk, block(index, TILE), :] = dot(
-                inverse_rows(index), mixed_near[...]).astype(half_type)
-
-        def far_tile(index):
-            far_cols[chunk, block(index, TILE), :] = dot(
-                inverse_rows(index), mixed_far[...]).astype(half_type)
-
-        def taps_tile(index):
-            band = block(index, TILE)
-            partial[chunk, band, :] = dot(inverse[band, :], mixed_taps[...]).astype(half_type)
-
-        loop(0, half_len // TILE, near_tile)
+        spectrum = butterfly(dot(forward[half], near[chunk, 0]), dot(forward[half], near[chunk, 1]))
+        for at in range(4):
+            near_spec[at] = spectrum[at]
+        unmix(mixed_near,
+              *times(spectrum[:2], (taps_spec[0], taps_spec[1])),
+              *times(spectrum[2:], (taps_spec[2], taps_spec[3])))
+        own_half = pl.ds(pl.multiple_of(half * quarter, quarter), quarter)
+        for parity in range(2):
+            near_cols[chunk, parity] = dot(
+                inverse[own_half, :], mixed_near[parity]).astype(jnp.bfloat16)
         back_near_way.start(chunk)
         cross_way.arrive(chunk)
         far_way.arrive(chunk)
-
-        def far_frequencies(index):
-            upper, lower, band = places(index)
-            early_real, early_imag = parts(dot(forward[0, band, :], whole[chunk, first, :]))
-            late_real, late_imag = parts(dot(forward[1, band, :], whole[chunk, second, :]))
-            near_real, near_imag = parts(near_spec[band, :])
-            part_real, part_imag = early_real * keep + late_real, early_imag * keep + late_imag
-            mixed_taps[upper, :] = (part_real * near_real + part_imag * near_imag).astype(half_type)
-            mixed_taps[lower, :] = (
-                (part_imag * near_real - part_real * near_imag) * sign).astype(half_type)
-            far_real, far_imag = early_real + late_real, early_imag + late_imag
-            taps_real, taps_imag = parts(taps_spec[band, :])
-            taps_imag = taps_imag * sign
-            mixed_far[upper, :] = (far_real * taps_real + far_imag * taps_imag).astype(half_type)
-            mixed_far[lower, :] = (far_imag * taps_real - far_real * taps_imag).astype(half_type)
-
-        loop(0, seq_len // TILE, far_frequencies)
-        loop(0, (2 - half) * (half_len // TILE), taps_tile)
+        early_spec = butterfly(*(dot(forward[0], whole[chunk, parity, first, :]) for parity in (0, 1)))
+        late_spec = butterfly(*(dot(forward[1], whole[chunk, parity, second, :]) for parity in (0, 1)))
+        wide = [one + two for one, two in zip(early_spec, late_spec)]
+        some = [one * keep + two for one, two in zip(early_spec, late_spec)]
+        unmix(mixed_far,
+              *times_conjugate(wide[:2], (taps_spec[0], taps_spec[1])),
+              *times_conjugate(wide[2:], (taps_spec[2], taps_spec[3])))
+        real, imag = times_conjugate(some[:2], (near_spec[0], near_spec[1]))
+        mirror_real, mirror_imag = times_conjugate(some[2:], (near_spec[2], near_spec[3]))
+        unmix(mixed_taps, real, imag * sign, mirror_real, mirror_imag * sign)
+
+        def taps_tile(index):
+            band = block(index, quarter)
+            for parity in range(2):
+                partial[chunk, parity, band, :] = dot(
+                    inverse[band, :], mixed_taps[parity]).astype(jnp.bfloat16)
+
+        loop(0, 2 - half, taps_tile)
         reduce_each(chunk, lambda copy: copy.start())
 
         @pl.when(chunk > 0)
         def _():
             finish(chunk - 1)
 
-        loop(0, half_len // TILE, far_tile)
+        for parity in range(2):
+            far_cols[chunk, parity] = dot(
+                inverse[own_half, :], mixed_far[parity]).astype(jnp.bfloat16)
         back_far_way.start(chunk)
 
     loop(0, mine, work)
@@ -369,7 +407,8 @@
     def _():
         loop(0, most, summed_cross_way.arrive)
 
-    filter_grad_ref[...] = summed_rows[0].astype(jnp.float32)
+    sums_ref[0] = summed_rows[0]
+    sums_ref[1] = jnp.zeros_like(summed_rows[1])
 
     @pl.when(early)
     def _():
@@ -381,7 +420,7 @@
         def _():
             loop(0, most, summed_way.arrive)
 
-        filter_grad_ref[...] += summed_rows[1].astype(jnp.float32)
+        sums_ref[1] = summed_rows[1]
 
     def sent(chunk):
         for way in (taps_cross_way, taps_way, cross_way, near_way, far_way,
@@ -403,27 +442,30 @@
 
 
 def gate_kernel(gate, cot, rows, sums, out_ref, gate_grad_ref, values_grad_ref, filter_grad_ref):
-    conv = rows[0].astype(jnp.float32)
+    def whole(parted):
+        return dot(joining(2 * parted.shape[1]), parted.reshape(-1, parted.shape[2]))
+
+    conv = whole(rows[0])
     out_ref[...] = (gate[...].astype(jnp.float32) * conv).astype(jnp.bfloat16)
     gate_grad_ref[...] = (cot[...].astype(jnp.float32) * conv).astype(jnp.bfloat16)
-    values_grad_ref[...] = rows[1]
-    filter_grad_ref[...] = sums[...]
+    values_grad_ref[...] = whole(rows[1]).astype(jnp.bfloat16)
+    filter_grad_ref[...] = whole(sums[0]) + whole(sums[1])
 
 
 def gate_results(gate_input, cotangent, result_rows, sums):
     rows, channels = gate_input.shape
-    own_rows = sums.shape[0]
-    steps = own_rows // 8
-    block = pl.BlockSpec((rows // steps, channels), lambda i: (i, 0))
-    pair = pl.BlockSpec((2, rows // steps, channels), lambda i: (0, i, 0))
-    few = pl.BlockSpec((8, channels), lambda i: (i, 0))
+    own_rows = 2 * sums.shape[2]
+    width = 512
+    block = pl.BlockSpec((rows, width), lambda i: (0, i))
+    pair = pl.BlockSpec((2, 2, rows // 2, width), lambda i: (0, 0, 0, i))
+    few = pl.BlockSpec((2, 2, own_rows // 2, width), lambda i: (0, 0, 0, i))
     shape = jax.ShapeDtypeStruct((rows, channels), jnp.bfloat16)
     return pl.pallas_call(
         gate_kernel,
-        grid=(steps,),
+        grid=(channels // width,),
         in_specs=[block, block, pair, few],
-        out_specs=(block, block, block, few),
-        out_shape=(shape, shape, shape, jax.ShapeDtypeStruct(sums.shape, jnp.float32)),
+        out_specs=(block, block, block, pl.BlockSpec((own_rows, width), lambda i: (0, i))),
+        out_shape=(shape, shape, shape, jax.ShapeDtypeStruct((own_rows, channels), jnp.float32)),
         compiler_params=pltpu.CompilerParams(vmem_limit_bytes=60 * 2**20),
     )(gate_input, cotangent, result_rows, sums)
 
@@ -439,14 +481,14 @@
     outer = max(1, pair * OUTER_EIGHTHS // 8)
     inner = pair - outer
     most = max(outer, inner)
-    forward, inverse = odd_tables(seq_len)
+    forward, inverse, twist = odd_tables(seq_len)
     half, full = jnp.bfloat16, jnp.float32
-    whole = pltpu.VMEM((most, seq_len, WIDTH), half)
-    halves = pltpu.VMEM((most, seq_len // 2, WIDTH), half)
-    mix = pltpu.VMEM((2 * seq_len, WIDTH), half)
-    spec = pltpu.VMEM((2 * seq_len, WIDTH), full)
+    whole = pltpu.VMEM((most, 2, seq_len // 2, WIDTH), half)
+    halves = pltpu.VMEM((most, 2, seq_len // 4, WIDTH), half)
+    mix = pltpu.VMEM((2, seq_len, WIDTH), half)
+    spec = pltpu.VMEM((4, seq_len // 2, WIDTH), full)
     block = pltpu.VMEM((rows, channels), half)
-    pair_rows = pltpu.VMEM((2, rows, channels), half)
+    pair_rows = pltpu.VMEM((2, 2, rows // 2, channels), half)
     sems = pltpu.SemaphoreType.DMA((2, most, ctx // 2))
     groups = pltpu.SemaphoreType.DMA((2, most, dp))
     anywhere = pl.BlockSpec(memory_space=pl.ANY)
@@ -455,20 +497,20 @@
     result_rows, sums = pl.pallas_call(
         functools.partial(kernel, (ctx, dp, rows, seq_len, outer, inner)),
         out_shape=(
-            jax.ShapeDtypeStruct((2, rows, channels), half),
-            jax.ShapeDtypeStruct((own_rows, channels), full),
+            jax.ShapeDtypeStruct((2, 2, rows // 2, channels), half),
+            jax.ShapeDtypeStruct((2, 2, own_rows // 2, channels), half),
         ),
-        in_specs=[anywhere] * 6,
+        in_specs=[anywhere] * 7,
         out_specs=(vmem,) * 2,
         scratch_shapes=[
-            block, block, pltpu.VMEM((own_rows, channels), full),
+            block, block, block, pltpu.VMEM((own_rows, channels), full),
             pltpu.VMEM(forward.shape, half), pltpu.VMEM(inverse.shape, half),
-            pltpu.VMEM((own_rows, channels), half), pair_rows,
+            pltpu.VMEM(twist.shape, full), pltpu.VMEM((2, own_rows // 2, channels), half), pair_rows,
             halves, whole, whole, spec, spec, mix, mix, mix,
-            halves, halves, whole, pltpu.VMEM((most, dp, part, WIDTH), half),
-            pltpu.VMEM((most, part, WIDTH), half),
-            pair_rows, pltpu.VMEM((2, own_rows, channels), half),
-            pltpu.SemaphoreType.DMA((6,)), groups, groups,
+            halves, halves, whole, pltpu.VMEM((most, dp, 2, part // 2, WIDTH), half),
+            pltpu.VMEM((most, 2, part // 2, WIDTH), half),
+            pair_rows, pltpu.VMEM((2, 2, own_rows // 2, channels), half),
+            pltpu.SemaphoreType.DMA((7,)), groups, groups,
         ] + [sems] * 9,
         compiler_params=pltpu.CompilerParams(
             collective_id=0, has_side_effects=True, vmem_limit_bytes=58 * 2**20
@@ -476,7 +518,7 @@
         cost_estimate=pl.CostEstimate(
             flops=flops, bytes_accessed=16 * rows * channels, transcendentals=0
         ),
-    )(gate_input[0], values[0], cotangent[0], filter_taps, forward, inverse)
+    )(gate_input[0], values[0], cotangent[0], filter_taps, forward, inverse, twist)
     output, gate_grad, values_grad, filter_grad = gate_results(
         gate_input[0], cotangent[0], result_rows, sums
     )

time: 104 us -> 106 us (1.019)
  Pallas kernels: 103 us -> 105 us
    pallas_call x1, Pallas kernels: 4.59 us -> 7.15 us  [gate_results(): pl.pallas_call(gate_kernel, grid=(channels // width,), in_specs=[block, b...]
where the time goes in v4:
time: 106 us
  Pallas kernels  105 us (99%)
    pallas_call x1, Pallas kernels, in_one_kernel(): pl.pallas_call(functools.partial(kernel, (ctx, dp, rows, seq_len, outer,...  98.3 us
    pallas_call x1, Pallas kernels, gate_results(): pl.pallas_call(gate_kernel, grid=(channels // width,), in_specs=[block, b...  7.15 us

profile of v4, /device:TPU:0, one launch (start us, length us, event | category | flops | bytes accessed | tf_op | source)
XLA Modules:
  0.0 106.1 jit_solution(18124838854543500706)
XLA Ops:
  0.6 98.3 %shard_map.102 = (bf16[2,2,64,4096]{3,2,1,0:T(8,128)(2,1)}, bf16[2,2,16,4096]{3,2,1,0:T(8,128)(2,1)}) custom-call(bf16[128,4096]{1,0:T(8,128)(2,1)} %bitcast.6, bf16[128,4096]{1,0:T(8,128)(2,1)} %bitcast.10, bf16[128,4096]{1,0:T(8,128)(2,1)} %bitcast.8, f32[32,4096]{1,0:T(8,128)} %taps_hbm.1, bf16[2,1024,256]{2,1,0:T(8,128)(2,1)} %constant.6.clone.forward_hbm, ...), custom_call_target="tpu_custom_call" | custom-call | flops 12884901888 | bytes 8388608 | tf_op jit(solution)/shard_map/pallas_call | solution.py:497
  99.0 7.1 %shard_map.103 = (bf16[128,4096]{1,0:T(8,128)(2,1)}, bf16[128,4096]{1,0:T(8,128)(2,1)}, bf16[128,4096]{1,0:T(8,128)(2,1)}, f32[32,4096]{1,0:T(8,128)}) custom-call(bf16[128,4096]{1,0:T(8,128)(2,1)} %bitcast.7, bf16[128,4096]{1,0:T(8,128)(2,1)} %bitcast.9, bf16[2,2,64,4096]{3,2,1,0:T(8,128)(2,1)} %get-tuple-element.10.rows, ...), custom_call_target="tpu_custom_call" | custom-call | tf_op jit(solution)/shard_map/pallas_call | solution.py:463

commit v5 on v3

--- a/solution.py
+++ b/solution.py
@@ -213,9 +213,24 @@
     loads[3].wait()
 
     def send_signals(chunk):
-        near_way.start(chunk)
-        cross_way.start(chunk)
-        far_way.start(chunk)
+        def turn(offset):
+            @pl.when(chunk < count(peer_at(offset, True)))
+            def _():
+                cross_way.to(chunk, offset).start()
+
+            for way, shift in ((near_way, 1), (far_way, 2)):
+                there = lax.rem(offset + shift, side)
+
+                @pl.when(jnp.logical_and(there > 0, chunk < count(peer_at(there, False))))
+                def _(way=way, there=there):
+                    way.to(chunk, there).start()
+
+        loop(0, side, turn)
+
+        @pl.when(chunk < count(me))
+        def _():
+            near_way.own(chunk).start()
+            far_way.own(chunk).start()
 
     send_signals(0)
     loads[4].start()
@@ -414,13 +429,13 @@
     rows, channels = gate_input.shape
     own_rows = sums.shape[0]
     steps = own_rows // 8
-    block = pl.BlockSpec((rows // steps, channels), lambda i: (i, 0))
-    pair = pl.BlockSpec((2, rows // steps, channels), lambda i: (0, i, 0))
-    few = pl.BlockSpec((8, channels), lambda i: (i, 0))
+    block = pl.BlockSpec((rows // steps, channels // 2), lambda i, j: (i, j))
+    pair = pl.BlockSpec((2, rows // steps, channels // 2), lambda i, j: (0, i, j))
+    few = pl.BlockSpec((8, channels // 2), lambda i, j: (i, j))
     shape = jax.ShapeDtypeStruct((rows, channels), jnp.bfloat16)
     return pl.pallas_call(
         gate_kernel,
-        grid=(steps,),
+        grid=(steps, 2),
         in_specs=[block, block, pair, few],
         out_specs=(block, block, block, few),
         out_shape=(shape, shape, shape, jax.ShapeDtypeStruct(sums.shape, jnp.float32)),

time: 104 us -> 106 us (1.019)
  Pallas kernels: 103 us -> 105 us
    pallas_call x1, Pallas kernels: 4.59 us -> 6.52 us  [gate_results(): pl.pallas_call(gate_kernel, grid=(steps, 2), in_specs=[block, block, pair...]
where the time goes in v5:
time: 106 us
  Pallas kernels  105 us (99%)
    pallas_call x1, Pallas kernels, in_one_kernel(): pl.pallas_call(functools.partial(kernel, (ctx, dp, rows, seq_len, outer,...  98.8 us
    pallas_call x1, Pallas kernels, gate_results(): pl.pallas_call(gate_kernel, grid=(steps, 2), in_specs=[block, block, pair...  6.52 us

profile of v5, /device:TPU:0, one launch (start us, length us, event | category | flops | bytes accessed | tf_op | source)
XLA Modules:
  0.0 106.0 jit_solution(3414297576828158338)
XLA Ops:
  0.6 98.8 %shard_map.93 = (bf16[2,128,4096]{2,1,0:T(8,128)(2,1)}, f32[32,4096]{1,0:T(8,128)}) custom-call(bf16[128,4096]{1,0:T(8,128)(2,1)} %bitcast.6, bf16[128,4096]{1,0:T(8,128)(2,1)} %bitcast.10, bf16[128,4096]{1,0:T(8,128)(2,1)} %bitcast.8, f32[32,4096]{1,0:T(8,128)} %taps_hbm.1, bf16[2,2048,512]{2,1,0:T(8,128)(2,1)} %constant.4.clone.forward_hbm, ...), custom_call_target="tpu_custom_call" | custom-call | flops 12884901888 | bytes 8388608 | tf_op jit(solution)/shard_map/pallas_call | solution.py:470
  99.5 6.5 %shard_map.94 = (bf16[128,4096]{1,0:T(8,128)(2,1)}, bf16[128,4096]{1,0:T(8,128)(2,1)}, bf16[128,4096]{1,0:T(8,128)(2,1)}, f32[32,4096]{1,0:T(8,128)}) custom-call(bf16[128,4096]{1,0:T(8,128)(2,1)} %bitcast.7, bf16[128,4096]{1,0:T(8,128)(2,1)} %bitcast.9, bf16[2,128,4096]{2,1,0:T(8,128)(2,1)} %get-tuple-element.10.rows, f32[32,4096]{1,0:T(8,128)} %get-tuple-element.11.sums), custom_call_target="tpu_custom_call" | custom-call | tf_op jit(solution)/shard_map/pallas_call | solution.py:436

commit v6 on v3

--- a/solution.py
+++ b/solution.py
@@ -413,10 +413,10 @@
 def gate_results(gate_input, cotangent, result_rows, sums):
     rows, channels = gate_input.shape
     own_rows = sums.shape[0]
-    steps = own_rows // 8
+    steps = 2
     block = pl.BlockSpec((rows // steps, channels), lambda i: (i, 0))
     pair = pl.BlockSpec((2, rows // steps, channels), lambda i: (0, i, 0))
-    few = pl.BlockSpec((8, channels), lambda i: (i, 0))
+    few = pl.BlockSpec((own_rows // steps, channels), lambda i: (i, 0))
     shape = jax.ShapeDtypeStruct((rows, channels), jnp.bfloat16)
     return pl.pallas_call(
         gate_kernel,

time: 104 us -> 103 us (level)
  no operation moved by 1% of the time
where the time goes in v6:
time: 103 us
  Pallas kernels  102 us (99%)
    pallas_call x1, Pallas kernels, in_one_kernel(): pl.pallas_call(functools.partial(kernel, (ctx, dp, rows, seq_len, outer,...  98.2 us
    pallas_call x1, Pallas kernels, gate_results(): pl.pallas_call(gate_kernel, grid=(steps,), in_specs=[block, block, pair,...  3.76 us

profile of v6, /device:TPU:0, one launch (start us, length us, event | category | flops | bytes accessed | tf_op | source)
XLA Modules:
  0.0 102.6 jit_solution(16037122677691084296)
XLA Ops:
  0.6 98.2 %shard_map.93 = (bf16[2,128,4096]{2,1,0:T(8,128)(2,1)}, f32[32,4096]{1,0:T(8,128)}) custom-call(bf16[128,4096]{1,0:T(8,128)(2,1)} %bitcast.6, bf16[128,4096]{1,0:T(8,128)(2,1)} %bitcast.10, bf16[128,4096]{1,0:T(8,128)(2,1)} %bitcast.8, f32[32,4096]{1,0:T(8,128)} %taps_hbm.1, bf16[2,2048,512]{2,1,0:T(8,128)(2,1)} %constant.4.clone.forward_hbm, ...), custom_call_target="tpu_custom_call" | custom-call | flops 12884901888 | bytes 8388608 | tf_op jit(solution)/shard_map/pallas_call | solution.py:455
  98.9 3.8 %shard_map.94 = (bf16[128,4096]{1,0:T(8,128)(2,1)}, bf16[128,4096]{1,0:T(8,128)(2,1)}, bf16[128,4096]{1,0:T(8,128)(2,1)}, f32[32,4096]{1,0:T(8,128)}) custom-call(bf16[128,4096]{1,0:T(8,128)(2,1)} %bitcast.7, bf16[128,4096]{1,0:T(8,128)(2,1)} %bitcast.9, bf16[2,128,4096]{2,1,0:T(8,128)(2,1)} %get-tuple-element.10.rows, f32[32,4096]{1,0:T(8,128)} %get-tuple-element.11.sums), custom_call_target="tpu_custom_call" | custom-call | tf_op jit(solution)/shard_map/pallas_call | solution.py:421
